TPU v7x, 32 devices: a whole 2x2x4 slice. The times are simulated.
32 devices in a mesh: band: 2 (over x), tile: 8 (over z, y), bin: 2 (over core).
Axes of the slice: x: 2, y: 2, z: 4, core: 2. Of those that a mesh axis runs over, the one named last changes fastest.
Arguments:
- spectra: float32 [1296, 8192], P(None, ('band', 'tile', 'bin')), parts along dimension 1, may hold values from 0.25 to 2
- wind: float32 [2, 8192], P(None, ('band', 'tile', 'bin')), parts along dimension 1, may hold values from -5 to 5
- mask: int32 [64, 256], P(None, 'band'), parts along dimension 1, may hold values from 0 to 1, as said below
- dia_index: int32 [2, 2, 4, 1296], replicated, may hold values from 0 to 1295, as said below
- dia_weight: bfloat16 [2, 2, 4, 1296], replicated, may hold values from 0.099609375 to 0.5
- nl_coef: float32 [1296], replicated, may hold values from 0.01 to 0.1
Outputs:
- propagated: float32 [1296, 64, 256], P('bin', 'tile', 'band'), parts along dimension 2
There are 2 independent parts, one for each index of `band`. A program takes and returns all parts, laid end to end along the dimension named above; an argument that names none is the same for every part. Nothing has to cross between parts.
Inputs may be any that keep to these rules, and one draw needn't show every extreme that they name: `mask`: exactly 4096 cells are sea; at least one tile of 8 columns is entirely sea. `dia_index`: for each mirror, member and bin, the corners are frequencies f and f + 1 with f in 0..34 and directions d and d + 1 modulo 36: four different bins.
All inputs are finite; a program needn't handle non-finite values.
Results may differ from a plain program's by a relative error of at most 0.0011.
Values sent between devices are 32-bit elements; how exact they have to be, the bound alone decides.
No kernel may reach another device: no remote copies, remote signals or barrier semaphores. Data moves between devices by JAX's collectives and lax.ppermute only.
A program may use at most 128 MiB of HBM per device.

v0:
```python
import dataclasses
import functools
import math

import jax
import jax.numpy as jnp
import numpy as np
from jax import lax
from jax.experimental import pallas as pl
from jax.experimental.pallas import tpu as pltpu
from jax.sharding import PartitionSpec as P

NTH = 36
STEPS = 2
LANES = 128
ROWS = 256
RING = 40
FIRST = 160
COMMON = 192
VMEM_BYTES = 58 * 1024 * 1024
SIZES = (160, 176, 192, 208, 224, 240)
BATCH = 8

LAMBDA = 0.25
COEF_THREE = (1.0 + LAMBDA) ** (-4)
COEF_FOUR = (1.0 - LAMBDA) ** (-4)
COEF_BOTH = (1.0 - LAMBDA * LAMBDA) ** (-4)
CFL_LIMIT = 0.8
WIND_RATE = 0.2


def round_up(value, step):
    return -(-value // step) * step


def bin_tables(count_bins):
    bin_range = np.arange(count_bins)
    theta = 2.0 * math.pi * (bin_range % NTH) / NTH
    group_speed = CFL_LIMIT * 1.1 ** (-(bin_range // NTH).astype(np.float64))
    return np.cos(theta), np.sin(theta), group_speed


def stencil(courant):
    bend = (1.0 - courant * courant) / 6.0
    up = courant >= 0.0
    zero = np.zeros_like(courant)
    left = courant * np.where(up, -bend, zero)
    here = courant * (0.5 + 0.5 * courant + np.where(up, 2.0 * bend, -bend))
    right = courant * (0.5 - 0.5 * courant + np.where(up, -bend, 2.0 * bend))
    far = courant * np.where(up, zero, -bend)
    return np.stack([left, here - left, 1.0 + right - here, far - right, -far])


def source_kernel(plan, first_point, spectra_far, wind_far, index_far, weight_far, nl_far, tables_far, out,
                  spectra, wind, index, weight, nl_coef, tables, arrived, code, weight_pad, nl_pad, spaced, flat_t, low_t, matrix, inter, total, twice):
    count_bins, points = spectra.shape
    padded = flat_t.shape[1]
    chunks = padded // LANES
    rings = count_bins // NTH
    depth = spaced.shape[0]
    whole = count_bins // LANES
    rest = count_bins - whole * LANES
    pairs = [(index_far, index), (weight_far, weight), (nl_far, nl_coef), (wind_far, wind),
             (tables_far, tables), (spectra_far, spectra)]
    copies = [pltpu.make_async_copy(far, near, arrived.at[k]) for k, (far, near) in enumerate(pairs)]
    for copy in copies:
        copy.start()

    code[...] = jnp.zeros(code.shape, jnp.int32)
    weight_pad[...] = jnp.zeros(weight_pad.shape, jnp.float32)
    nl_pad[...] = jnp.zeros(nl_pad.shape, jnp.float32)
    for copy in copies:
        copy.wait()
    nl_pad[:, :count_bins] = nl_coef[...].reshape(1, count_bins)
    for mirror in range(2):
        for member in range(2):
            row = (mirror * 2 + member) * 4
            bins = index[mirror, member]
            ring = ((bins.astype(jnp.float32) + 0.5) * (1.0 / NTH)).astype(jnp.int32)
            lowest = jnp.minimum(jnp.minimum(ring[0:1], ring[1:2]), jnp.minimum(ring[2:3], ring[3:4]))
            direction = bins - ring * NTH
            code[row:row + 4, :count_bins] = jnp.where(ring == lowest, direction, direction + RING)
            code[16 + mirror * 2 + member:17 + mirror * 2 + member, :count_bins] = lowest
            weight_pad[row:row + 4, :count_bins] = weight[mirror, member].astype(jnp.float32)

    gap = jnp.zeros((RING - NTH, points), jnp.float32)
    for ring in range(rings):
        spaced[ring * RING:ring * RING + NTH, :] = spectra[ring * NTH:(ring + 1) * NTH, :]
        spaced[ring * RING + NTH:(ring + 1) * RING, :] = gap
    spaced[rings * RING:, :] = jnp.zeros((depth - rings * RING, points), jnp.float32)
    for half in range(points // LANES):
        span = slice(half * LANES, (half + 1) * LANES)
        for block in range(depth // LANES):
            lanes = slice(block * LANES, (block + 1) * LANES)
            low_t[span, lanes] = spaced[lanes, span].T.astype(jnp.bfloat16)
        for block in range(chunks):
            lanes = slice(block * LANES, (block + 1) * LANES)
            if block < whole:
                values = spectra[lanes, span]
            else:
                values = jnp.concatenate(
                    [spectra[whole * LANES:, span], jnp.zeros((LANES - rest, LANES), jnp.float32)], axis=0
                )
            flat_t[span, lanes] = values.T

    used = rings * RING
    matrix[used:, :] = jnp.zeros((depth - used, matrix.shape[1]), jnp.bfloat16)

    def members_of(chunk):
        lanes = slice(chunk * LANES, (chunk + 1) * LANES)
        wide = chunk * 4 * LANES
        place = lax.broadcasted_iota(jnp.int32, (RING, LANES), 0)
        patterns = []
        for pair in range(4):
            low = jnp.zeros((RING, LANES), jnp.float32)
            high = low
            for corner in range(4):
                r = pair * 4 + corner
                where = code[r:r + 1, lanes]
                amount = jnp.broadcast_to(weight_pad[r:r + 1, lanes], (RING, LANES))
                low = jnp.where(place == where, amount, low)
                high = jnp.where(place + RING == where, amount, high)
            lowest = jnp.broadcast_to(code[16 + pair:17 + pair, lanes], (8, LANES))
            patterns.append((low, high, lowest))
        members = [jnp.zeros((points, 2 * LANES), jnp.float32) for _ in range(2)]
        done = 0
        for ring in range(0, rings, 2):
            for pair in range(4):
                low, high, lowest = patterns[pair]
                parts = []
                for offset in range(2):
                    first = lowest == ring + offset
                    second = lowest == ring + offset - 1
                    for sub in range(0, RING, 8):
                        parts.append(
                            jnp.where(first, low[sub:sub + 8], jnp.where(second, high[sub:sub + 8], 0.0))
                        )
                matrix[ring * RING:(ring + 2) * RING, wide + pair * LANES:wide + (pair + 1) * LANES] = (
                    jnp.concatenate(parts, axis=0).astype(jnp.bfloat16)
                )
            ready = (ring + 2) * RING
            while done < depth and (ready >= done + ROWS or ready == used):
                size = min(ROWS, depth - done)
                for mirror in range(2):
                    members[mirror] = members[mirror] + jnp.dot(
                        low_t[:, done:done + size],
                        matrix[done:done + size, wide + mirror * 2 * LANES:wide + (mirror + 1) * 2 * LANES],
                        preferred_element_type=jnp.float32,
                    )
                done += size
        return members

    def interact(chunk, members):
        lanes = slice(chunk * LANES, (chunk + 1) * LANES)
        wide = chunk * 4 * LANES
        valid = min(LANES, count_bins - chunk * LANES)
        rows = slice(chunk * LANES, chunk * LANES + valid)
        values = flat_t[:, lanes]
        coef = nl_pad[:, lanes]
        turned = []
        for mirror in range(2):
            third = members[mirror][:, :LANES]
            fourth = members[mirror][:, LANES:]
            interaction = coef * (
                values * values * (COEF_THREE * third + COEF_FOUR * fourth)
                - 2.0 * COEF_BOTH * values * third * fourth
            )
            turned.append([interaction[half * LANES:(half + 1) * LANES].T for half in range(points // LANES)])
        for half in range(points // LANES):
            span = slice(half * LANES, (half + 1) * LANES)
            for mirror in range(2):
                low = turned[mirror][half].astype(jnp.bfloat16)
                for member in range(2):
                    start = wide + (mirror * 2 + member) * LANES
                    inter[start:start + LANES, span] = low
            drive = jnp.maximum(
                wind[0:1, span] * tables[0, rows, :] + wind[1:2, span] * tables[1, rows, :], 0.0
            )
            here = spectra[rows, span]
            both = (turned[0][half] + turned[1][half])[:valid]
            total[rows, span] = here + WIND_RATE * drive * here - 2.0 * both

    previous = None
    for chunk in range(chunks):
        members = members_of(chunk)
        if previous is not None:
            interact(chunk - 1, previous)
        previous = members
    interact(chunks - 1, previous)
    added = 0
    packed = 0
    owners = [(side, member) for side in range(plan.halves) for member in range(plan.members)]
    for start in range(0, used, ROWS):
        size = min(ROWS, used - start)
        spaced[start:start + size, :] = jnp.dot(
            matrix[start:start + size, :], inter[...], preferred_element_type=jnp.float32
        )
        while added < rings and added * RING + NTH <= start + size:
            total[added * NTH:(added + 1) * NTH, :] += spaced[added * RING:added * RING + NTH, :]
            added += 1
        while packed < len(owners):
            side, member = owners[packed]
            if min(side * plan.half_bins + (member + 1) * plan.per, count_bins) > added * NTH:
                break
            pack_payload(plan, first_point, total, out, twice, side, member)
            packed += 1


def pack_payload(plan, first_point, total, out, twice, side, member):
    points = total.shape[1]
    main, rest, fold = plan.main, plan.rest, plan.fold
    lane = lax.broadcasted_iota(jnp.int32, (1, LANES), 1)
    first = side * plan.half_bins + member * plan.per
    valid = min(main, plan.half_bins - member * plan.per)
    slot = (side * plan.members + member) % 2
    for half in range(points // LANES):
        values = total[first:first + valid, half * LANES:(half + 1) * LANES]
        if valid < LANES:
            values = jnp.concatenate([values, jnp.zeros((LANES - valid, LANES), jnp.float32)], axis=0)
        turned = values.T
        twice[slot, half * LANES:(half + 1) * LANES, :] = turned
        twice[slot, points + half * LANES:points + (half + 1) * LANES, :] = turned
    for part in range(plan.parts):
        owner = (part * plan.members + member) * plan.halves + side
        begin = lax.rem(first_point[part], points)
        for low, high in ((0, FIRST), (FIRST, COMMON), (COMMON, points)):
            row = plan.row_of(low)
            out[owner, row:row + high - low, :] = twice[slot, pl.ds(begin + low, high - low), :]
        if not rest:
            continue
        shift = lax.rem(begin, LANES)
        swapped = begin >= LANES
        near = pltpu.roll(total[first + main:first + main + rest, :LANES], lax.rem(LANES - shift, LANES), 1)
        away = pltpu.roll(total[first + main:first + main + rest, LANES:], lax.rem(LANES - shift, LANES), 1)
        keep = (lane < LANES - shift) != swapped
        lead = jnp.where(keep, near, away)
        tail = jnp.where(keep, away, near)
        moved = pltpu.roll(tail, LANES // 2, 1)
        out[owner, FIRST:FIRST + rest, :] = lead
        out[owner, FIRST + rest:FIRST + rest + fold, :] = jnp.where(lane < LANES // 2, tail[:fold], moved[rest - fold:])
        out[owner, rest + fold + COMMON:rest + 2 * fold + COMMON, :] = jnp.where(
            lane < LANES // 2, moved[:fold], tail[rest - fold:]
        )


def source_terms(plan, first_point, spectra, wind, index, weight, nl_coef):
    count_bins, points = spectra.shape
    padded = round_up(count_bins, LANES)
    depth = round_up(count_bins // NTH * RING, LANES)
    cosine, sine, _ = bin_tables(count_bins)
    tables = np.stack([cosine, sine]).astype(np.float32)[:, :, None] * np.ones((1, 1, LANES), np.float32)
    smem = pl.BlockSpec(memory_space=pltpu.SMEM)
    vmem = pl.BlockSpec(memory_space=pltpu.VMEM)
    operands = (spectra, wind, index, weight, nl_coef, jnp.asarray(tables))
    return pl.pallas_call(
        functools.partial(source_kernel, plan),
        out_shape=jax.ShapeDtypeStruct((plan.group, plan.rows(points), LANES), jnp.float32),
        in_specs=[smem] + [pl.BlockSpec(memory_space=pl.ANY)] * len(operands),
        out_specs=vmem,
        scratch_shapes=[pltpu.VMEM(operand.shape, operand.dtype) for operand in operands] + [
            pltpu.SemaphoreType.DMA((len(operands),)),
            pltpu.VMEM((24, padded), jnp.int32),
            pltpu.VMEM((16, padded), jnp.float32),
            pltpu.VMEM((1, padded), jnp.float32),
            pltpu.VMEM((depth, points), jnp.float32),
            pltpu.VMEM((points, padded), jnp.float32),
            pltpu.VMEM((points, depth), jnp.bfloat16),
            pltpu.VMEM((depth, 4 * padded), jnp.bfloat16),
            pltpu.VMEM((4 * padded, points), jnp.bfloat16),
            pltpu.VMEM((padded, points), jnp.float32),
            pltpu.VMEM((2, 2 * points, LANES), jnp.float32),
        ],
        compiler_params=pltpu.CompilerParams(vmem_limit_bytes=VMEM_BYTES),
        cost_estimate=pl.CostEstimate(
            flops=4 * depth * 4 * padded * points, bytes_accessed=8 * count_bins * points, transcendentals=0
        ),
        name="source_terms",
    )(first_point, *operands)


def ranks_kernel(plan, sea_total, rank, mask, triangle, need, first_point, floor, rel):
    columns, latitudes = mask.shape
    sea = mask[...].astype(jnp.float32).astype(jnp.bfloat16)

    def product(left, right):
        return jnp.dot(left, right, preferred_element_type=jnp.float32)

    upto = product(sea, triangle[...])
    counts = lax.dot_general(
        jnp.ones((8, latitudes), jnp.bfloat16), sea, (((1,), (1,)), ((), ())), preferred_element_type=jnp.float32
    )
    row = lax.broadcasted_iota(jnp.int32, (columns, columns), 0)
    col = lax.broadcasted_iota(jnp.int32, (columns, columns), 1)
    before_row = product(counts.astype(jnp.bfloat16), jnp.where(row < col, 1.0, 0.0).astype(jnp.bfloat16))
    before_col = jnp.sum(product(jnp.where(col < row, 1.0, 0.0).astype(jnp.bfloat16), sea), axis=1, keepdims=True)
    lane = lax.broadcasted_iota(jnp.int32, (1, columns), 1)
    most = 0
    chosen = 0
    for p in range(plan.parts):
        begin = (p * (columns // plan.parts) - plan.halo) % columns
        inside = (lane + (columns - begin)) & (columns - 1)
        start = jnp.sum(jnp.where(lane == begin, before_row[:1], 0.0)).astype(jnp.int32)
        held = jnp.sum(jnp.where(inside < plan.window, counts[:1], 0.0)).astype(jnp.int32)
        wanted = (held + lax.rem(start, plan.group) + plan.group - 1) // plan.group
        first = jnp.where(wanted * plan.group <= sea_total, start // plan.group, 0)
        first_point[p] = first
        most = jnp.maximum(most, wanted)
        chosen = jnp.where(rank[0] // (plan.halves * plan.members) == p, first, chosen)
    need[0] = most

    def placed(before):
        place = before.astype(jnp.int32) - chosen * plan.group
        place = jnp.where(place < 0, place + sea_total, place)
        return place

    floor[...] = placed(before_row[:1])
    rel[...] = jnp.where(mask[...] == 1, upto.astype(jnp.int32) - 1 + placed(before_col), -1)


def sea_ranks(plan, sea_total, rank, mask):
    columns, latitudes = mask.shape
    smem = pl.BlockSpec(memory_space=pltpu.SMEM)
    vmem = pl.BlockSpec(memory_space=pltpu.VMEM)
    return pl.pallas_call(
        functools.partial(ranks_kernel, plan, sea_total),
        out_shape=[
            jax.ShapeDtypeStruct((1,), jnp.int32),
            jax.ShapeDtypeStruct((plan.parts,), jnp.int32),
            jax.ShapeDtypeStruct((1, columns), jnp.int32),
            jax.ShapeDtypeStruct((columns, latitudes), jnp.int32),
        ],
        in_specs=[smem, vmem, vmem],
        out_specs=[smem, smem, vmem, vmem],
        name="sea_ranks",
    )(rank, mask, jnp.asarray(np.triu(np.ones((latitudes, latitudes))), jnp.bfloat16))


def propagate_kernel(plan, slots, rank, base, got, rel, table, out, taps, arrived, ranked, extra, lined, pick, sea, starts):
    group = got.shape[0]
    columns = plan.window
    all_columns = rel.shape[0]
    shares = plan.halves * plan.members
    begin = rank[0] // shares * (all_columns // plan.parts) + (all_columns - plan.halo)
    copy = pltpu.make_async_copy(table.at[lax.rem(rank[0], shares)], taps, arrived)
    copy.start()
    per, columns_tile, halo = plan.per, plan.columns_tile, plan.halo
    main, rest, fold = plan.main, plan.rest, plan.fold
    half_lanes = lax.broadcasted_iota(jnp.int32, (1, LANES), 1) < LANES // 2
    rest_rows = round_up(rest, 8)

    fill = jnp.zeros((LANES // 2 - rest, LANES), jnp.float32)

    def turned_rest(owner):
        near = got[owner, FIRST + rest:FIRST + rest + fold, :]
        first = near
        second = pltpu.roll(near, LANES // 2, 1)
        if slots > COMMON:
            away = got[owner, rest + fold + COMMON:rest + 2 * fold + COMMON, :]
            first = jnp.where(half_lanes, first, pltpu.roll(away, LANES // 2, 1))
            second = jnp.where(half_lanes, second, away)
        return jnp.concatenate([got[owner, FIRST:FIRST + rest, :], fill, first[:rest - fold], second, fill], axis=0).T

    def order(step, carry):
        owners = [step * BATCH + k for k in range(BATCH)]
        turned = [turned_rest(owner) for owner in owners] if rest else []
        for owner in owners:
            for low, high in ((0, FIRST), (FIRST, min(slots, COMMON)), (COMMON, slots)):
                if high > low:
                    row = plan.row_of(low)
                    ranked[pl.ds(owner + low * group, high - low, stride=group), :] = got[
                        owner, row:row + high - low, :
                    ]
        for owner, values in zip(owners, turned):
            extra[pl.ds(owner, LANES, stride=group), :] = values
        return carry

    lax.fori_loop(0, group // BATCH, order, 0)

    rank_tiles = ranked.shape[0] // LANES
    padded = lined.shape[0]
    main_rows = round_up(main, 8)

    def line_up(step, carry):
        starts = [pl.multiple_of(step * (2 * LANES) + k * LANES, LANES) for k in range(2)]
        turned = [ranked[pl.ds(start, LANES), :].T[:main_rows] for start in starts]
        for start, values in zip(starts, turned):
            lined[:main_rows, pl.ds(start, LANES)] = values
            if not rest and main % 8:
                lined[main_rows - 8:main_rows, pl.ds(start, LANES)] = values[main - 8:main]
        return carry

    lax.fori_loop(0, rank_tiles // 2, line_up, 0)

    def line_up_rest(both, step, carry):
        starts = [pl.multiple_of(step * (2 * LANES) + k * LANES, LANES) for k in range(2)]
        turned = [extra[pl.ds(start, LANES), :].T for start in starts]
        for start, values in zip(starts, turned):
            for half in range(2 if both else 1):
                lanes = pl.ds(start + half * group * LANES, LANES)
                lined[main:main + rest_rows - 8, lanes] = values[half * LANES // 2:half * LANES // 2 + rest_rows - 8]
                lined[main + rest_rows - 8:main + rest_rows, lanes] = values[
                    half * LANES // 2 + rest - 8:half * LANES // 2 + rest
                ]
        return carry

    if rest:
        second = (rank_tiles - group) // 2
        lax.fori_loop(0, second, functools.partial(line_up_rest, True), 0)
        lax.fori_loop(second, group // 2, functools.partial(line_up_rest, False), 0)
    lined[:, rank_tiles * LANES:] = jnp.zeros((padded, 2 * LANES), jnp.float32)

    for column in range(columns):
        source = (begin + column) & (all_columns - 1)
        starts[column] = base[0, source]
        row = jnp.broadcast_to(rel[pl.ds(source, 1), :], (8, LANES))
        pick[column] = row & (LANES - 1)
        sea[column] = jnp.where(row >= 0, 1.0, 0.0)

    lane = lax.broadcasted_iota(jnp.int32, (8, LANES), 1)
    copy.wait()

    def bins_step(tile, carry):
        span = pl.ds(pl.multiple_of(tile * 8, 8), 8)
        first_bin = jnp.minimum(tile * 8, per - 8)
        tap = [jnp.broadcast_to(taps[span, k:k + 1], (8, LANES)) for k in range(10)]
        x_up = tap[0] != 0.0
        x_far = jnp.where(x_up, tap[0], tap[4])
        y_up = tap[5] != 0.0
        far_lane = jnp.where(y_up, lane - 2, lane + 2)
        y_far = jnp.where((far_lane >= 0) & (far_lane < LANES), jnp.where(y_up, tap[5], tap[9]), 0.0)
        far_lane = far_lane & (LANES - 1)
        y_left = jnp.where(lane >= 1, tap[6], 0.0)
        y_right = jnp.where(lane < LANES - 1, tap[8], 0.0)

        def expanded(column):
            place = starts[column]
            offset = place & (LANES - 1)
            start = pl.multiple_of(place - offset, LANES)
            low = lined[span, pl.ds(start, LANES)]
            high = lined[span, pl.ds(start + LANES, LANES)]
            both = jnp.where(lane >= offset, low, high)
            return jnp.take_along_axis(both, pick[column], axis=1) * sea[column]

        def store(result, column):
            owner, place = divmod(column - halo, columns_tile)
            start = (owner * per + first_bin) * columns_tile + place
            out[pl.ds(start, 8, stride=columns_tile), :] = result

        def sweep(values, column):
            left_two, left, here, right, right_two = neighbours(values, column)
            value = tap[2] * here + tap[1] * left + tap[3] * right + x_far * jnp.where(x_up, left_two, right_two)
            value = value * sea[column]
            moved = (
                tap[7] * value + y_left * pltpu.roll(value, 1, 1) + y_right * pltpu.roll(value, LANES - 1, 1)
                + y_far * jnp.take_along_axis(value, far_lane, axis=1)
            )
            return moved * sea[column]

        reach = halo // STEPS
        first = {}

        def neighbours(values, column):
            return [values[(column + k) % columns] for k in range(-2, 3)]

        for column in range(columns):
            first[column] = expanded(column)
        middle = {column: sweep(first, column) for column in range(reach, columns - reach)}
        results = {column: sweep(middle, column) for column in range(halo, columns - halo)}
        for column, result in results.items():
            store(result, column)
        return carry

    lax.fori_loop(0, -(-per // 8), bins_step, 0)


def propagate(plan, slots, rank, base, got, rel, table):
    columns = plan.window
    padded = round_up(plan.per, 8)
    ranks = plan.group * slots
    smem = pl.BlockSpec(memory_space=pltpu.SMEM)
    vmem = pl.BlockSpec(memory_space=pltpu.VMEM)
    return pl.pallas_call(
        functools.partial(propagate_kernel, plan, slots),
        out_shape=jax.ShapeDtypeStruct(((columns - 2 * plan.halo) * plan.per, LANES), jnp.float32),
        in_specs=[smem, smem, vmem, vmem, pl.BlockSpec(memory_space=pl.ANY)],
        out_specs=vmem,
        scratch_shapes=[
            pltpu.VMEM((padded, LANES), jnp.float32),
            pltpu.SemaphoreType.DMA,
            pltpu.VMEM((ranks, LANES), jnp.float32),
            pltpu.VMEM((LANES * plan.group if plan.rest else 8, LANES), jnp.float32),
            pltpu.VMEM((padded, ranks + 2 * LANES), jnp.float32),
            pltpu.VMEM((columns, 8, LANES), jnp.int32),
            pltpu.VMEM((columns, 8, LANES), jnp.float32),
            pltpu.SMEM((columns,), jnp.int32),
        ],
        compiler_params=pltpu.CompilerParams(vmem_limit_bytes=VMEM_BYTES),
        name="propagate",
    )(rank, base, got, rel, table)


@dataclasses.dataclass(frozen=True)
class Plan:
    tiles: int
    halves: int
    parts: int
    half_bins: int
    columns: int

    @property
    def group(self):
        return self.tiles * self.halves

    @property
    def members(self):
        return self.tiles // self.parts

    @property
    def per(self):
        return -(-self.half_bins // self.members)

    @property
    def main(self):
        return min(self.per, LANES)

    @property
    def rest(self):
        return self.per - self.main

    @property
    def fold(self):
        return -(-self.rest // 2)

    @property
    def columns_tile(self):
        return self.columns // self.tiles

    @property
    def halo(self):
        return 2 * STEPS if self.parts > 1 else 0

    @property
    def window(self):
        return self.columns // self.parts + 2 * self.halo

    def row_of(self, point):
        return point + (self.rest + self.fold if point >= FIRST else 0) + (self.fold if point >= COMMON else 0)

    def rows(self, slots):
        return self.rest + (2 if slots > COMMON else 1) * self.fold + slots


def shards(spectra, wind, mask, dia_index, dia_weight, nl_coef):
    count_bins, points = spectra.shape
    columns, latitudes = mask.shape
    plan = Plan(
        tiles=lax.axis_size("tile"), halves=lax.axis_size("bin"), parts=2,
        half_bins=count_bins // lax.axis_size("bin"), columns=columns,
    )
    members, parts = plan.members, plan.parts
    sea_total = plan.group * points
    tile_rank = lax.axis_index("tile")

    rank = (
        tile_rank // members * (plan.halves * members) + lax.axis_index("bin") * members + tile_rank % members
    ).astype(jnp.int32).reshape(1)
    need, first_point, floor, rel = sea_ranks(plan, sea_total, rank, mask)
    wanted = need
    bands = lax.axis_size("band")
    for step in range(1, bands):
        wanted = jnp.maximum(
            wanted, lax.ppermute(need, "band", [(band, (band + step) % bands) for band in range(bands)])
        )
    wanted = wanted[0]

    payload = source_terms(plan, first_point, spectra, wind, dia_index, dia_weight, nl_coef)

    cosine, sine, speed = bin_tables(count_bins)
    weights = np.concatenate([stencil(speed * cosine), stencil(speed * sine)])
    table = np.zeros((plan.halves, members, round_up(plan.per, 8), LANES), np.float32)
    for side in range(plan.halves):
        for member in range(members):
            valid = max(0, min(plan.per, plan.half_bins - member * plan.per))
            begin = side * plan.half_bins + member * plan.per
            table[side, member, :valid, :10] = weights[:, begin:begin + valid].T
            if plan.per % 8:
                table[side, member, -8:] = table[side, member, plan.per - 8:plan.per].copy()
    table = jnp.asarray(table.reshape((plan.halves * members,) + table.shape[2:]))

    def with_slots(slots):
        def run(payload, rank, floor, rel, table):
            got = lax.all_to_all(
                payload[:, :plan.rows(slots)], ("tile", "bin"), split_axis=0, concat_axis=0, tiled=True
            )
            return propagate(plan, slots, rank, floor, got, rel, table)

        return run

    sizes = [size for size in SIZES if size < points] + [points]
    choice = sum((wanted > size).astype(jnp.int32) for size in sizes[:-1])
    moved = lax.switch(choice, [with_slots(size) for size in sizes], payload, rank, floor, rel, table)
    result = lax.all_to_all(
        moved.reshape(members, plan.per, plan.columns_tile, latitudes), "tile", split_axis=0, concat_axis=0,
        axis_index_groups=[list(range(p * members, (p + 1) * members)) for p in range(parts)], tiled=True,
    ).reshape(members * plan.per, plan.columns_tile, latitudes)
    return result[:plan.half_bins]


def solution(mesh):
    in_specs = (
        P(None, ("band", "tile", "bin")),
        P(None, ("band", "tile", "bin")),
        P(None, "band"),
        P(),
        P(),
        P(),
    )
    out_specs = P("bin", "tile", "band")
    return jax.shard_map(shards, mesh=mesh, in_specs=in_specs, out_specs=out_specs, check_vma=False)
```

profile of v0, /device:TPU:0, one launch (start us, length us, event | category | flops | bytes accessed | tf_op | source)
XLA Modules:
  0.0 125.3 jit_solution(12913518241521423786)
XLA Ops:
  0.0 1.7 %sea_ranks.1 = (s32[1]{0:T(128)}, s32[2]{0:T(128)}, s32[1,64]{1,0:T(1,128)S(1)}, s32[64,128]{1,0:T(8,128)S(1)}) custom-call(s32[1]{0:T(128)} %bitcast.rank, s32[64,128]{1,0:T(8,128)} %mask.1, bf16[128,128]{1,0:T(8,128)(2,1)} %constant.63.clone.triangle), custom_call_target="tpu_custom_call" | custom-call | tf_op jit(solution)/shard_map/sea_ranks/pallas_call | solution.py:324
  1.7 3.0 %collective-permute-start = (s32[1]{0:T(128)}, s32[1]{0:T(128)}, u32[]{:S(2)}, u32[]{:S(2)}) collective-permute-start(s32[1]{0:T(128)} %get-tuple-element.122), channel_id=1, source_target_pairs={{0,16},{16,0},{1,17},{17,1},{2,18},{18,2},{3,19},{19,3},{4,20},{20... | collective-permute-start | bytes 20 | tf_op jit(solution)/shard_map/ppermute | solution.py:572
  4.7 0.0 copy-start
  4.7 15.3 %source_terms.1 = f32[16,324,128]{2,1,0:T(8,128)S(1)} custom-call(s32[2]{0:T(128)} %get-tuple-element.123.first_point, f32[1296,256]{1,0:T(8,128)} %spectra_far.1, f32[2,256]{1,0:T(2,128)} %wind_far.1, s32[2,2,4,1296]{3,2,1,0:T(4,128)} %index_far.1, bf16[2,2,4,1296]{3,2,1,0:T(4,128)(2,1)} %weight_far.1, f32[1296]{0:T(1024)} %nl_far.1, ...), custom_call_target="tpu_custom_call" | custom-call | flops 8858370048 | bytes 2654208 | tf_op jit(solution)/shard_map/source_terms/pallas_call | solution.py:255
  20.0 0.0 collective-permute-done
  21.3 0.0 copy-done
  21.3 66.9 %conditional.1 = (f32[5184,128]{1,0:T(8,128)S(1)}) conditional(s32[]{:T(128)} %bitcast.1, (f32[16,324,128]{2,1,0:T(8,128)S(1)}, s32[1]{0:T(128)}, s32[1,64]{1,0:T(1,128)S(1)}, s32[64,128]{1,0:T(8,128)S(1)}, f32[8,168,128]{2,1,0:T(8,128)S(1)}) %tuple.34, (f32[16,324,128]{2,1,0:T(8,128)S(1)}, s32[1]{0:T(128)}, ...), branch_computations={%region_0.1_spmd, %region_1.2_spmd, %region_2.3_spmd, %region_3.4_... | conditional | bytes 10092552 | solution.py:601
  21.6 0.1 slice.14
  21.7 52.0 %all_to_all.35.got = f32[16,243,128]{2,1,0:T(8,128)} all-to-all(f32[16,243,128]{2,1,0:T(8,128)S(1)} %slice.14), channel_id=1, replica_groups=mesh['band'=2,'tile'=8,'bin'=2] {'tile','bin'}, dimensions={0} | all-to-all | bytes 3981312 | tf_op jit(solution)/shard_map/cond/branch_2_fun/all_to_all | solution.py:592
  73.7 14.3 %propagate.9 = f32[5184,128]{1,0:T(8,128)S(1)} custom-call(s32[1]{0:T(128)} %get-tuple-element.93.rank, s32[1,64]{1,0:T(1,128)S(1)} %get-tuple-element.94.base, f32[16,243,128]{2,1,0:T(8,128)} %all_to_all.35.got, s32[64,128]{1,0:T(8,128)S(1)} %get-tuple-element.96.rel, f32[8,168,128]{2,1,0:T(8,128)S(1)} %get-tuple-element.97.table), custom_call_target="tpu_custom_call" | custom-call | tf_op jit(solution)/shard_map/cond/branch_2_fun/propagate/pallas_call | solution.py:482
  88.3 35.5 %all_to_all.40 = f32[4,162,8,128]{3,2,1,0:T(8,128)S(1)} all-to-all(f32[4,162,8,128]{3,2,1,0:T(8,128)S(1)} %bitcast.4), channel_id=1, replica_groups={{0,2,4,6},{8,10,12,14},{1,3,5,7},{9,11,13,15},{16,18,20,22},{24,26,28,3..., dimensions={0} | all-to-all | bytes 5308416 | tf_op jit(solution)/shard_map/all_to_all | solution.py:602
  123.8 1.5 %copy.18 = f32[648,8,128]{2,1,0:T(8,128)} copy(f32[648,8,128]{2,1,0:T(8,128)S(1)} %bitcast.5) | data formatting | bytes 5308416
Async XLA Ops:
  1.7 18.3 %collective-permute-start = (s32[1]{0:T(128)}, s32[1]{0:T(128)}, u32[]{:S(2)}, u32[]{:S(2)}) collective-permute-start(s32[1]{0:T(128)} %get-tuple-element.122), channel_id=1, source_target_pairs={{0,16},{16,0},{1,17},{17,1},{2,18},{18,2},{3,19},{19,3},{4,20},{20... | collective-permute-start | bytes 20 | tf_op jit(solution)/shard_map/ppermute | solution.py:572
  4.7 16.6 %copy-start = (f32[8,168,128]{2,1,0:T(8,128)S(1)}, f32[8,168,128]{2,1,0:T(8,128)}, u32[]{:S(2)}) copy-start(f32[8,168,128]{2,1,0:T(8,128)} %constant.65.clone) | copy-start | bytes 2064388
where the time goes:
time: 126 us; the launch traced here: 125 us
  blocking collectives  87.6 us (70%)
  Pallas kernels  31.3 us (25%)
  starting transfers between devices  3 us (2%)
  local copies, waits for them, and re-layouts  1.64 us (1%)
  between operations  1.33 us (1%)
    all_to_all x1, blocking collectives, run(): lax.all_to_all(payload[:, :plan.rows(slots)], ('tile', 'bin'), split_axis...  52 us
    all_to_all x1, blocking collectives, shards(): lax.all_to_all(moved.reshape(members, plan.per, plan.columns_tile, latitu...  35.5 us
    pallas_call x1, Pallas kernels, source_terms(): pl.pallas_call(functools.partial(source_kernel, plan), out_shape=jax.Shap...  15.3 us
    pallas_call x1, Pallas kernels, propagate(): pl.pallas_call(functools.partial(propagate_kernel, plan, slots), out_shap...  14.3 us
    ppermute x1, starting transfers between devices, shards(): lax.ppermute(need, 'band', [(band, (band + step) % bands) for band in ran...  3 us
  transfers between devices with their start and end apart: 1, of which 0 were waited for; matrix products, arithmetic and copies ran while one was open for 0% of the time, Pallas kernels for 12%

commit v1 on v0

--- a/solution.py
+++ b/solution.py
@@ -120,24 +120,31 @@
                 amount = jnp.broadcast_to(weight_pad[r:r + 1, lanes], (RING, LANES))
                 low = jnp.where(place == where, amount, low)
                 high = jnp.where(place + RING == where, amount, high)
-            lowest = jnp.broadcast_to(code[16 + pair:17 + pair, lanes], (8, LANES))
-            patterns.append((low, high, lowest))
+            lowest = jnp.broadcast_to(code[16 + pair:17 + pair, lanes], (16, LANES)).astype(jnp.float32)
+            empty = jnp.zeros((RING, LANES), jnp.float32)
+            patterns.append((
+                lowest.astype(jnp.bfloat16),
+                [
+                    jnp.concatenate(rings_of, axis=0).astype(jnp.bfloat16)
+                    for rings_of in ((low, high), (empty, low), (high, empty))
+                ],
+            ))
         members = [jnp.zeros((points, 2 * LANES), jnp.float32) for _ in range(2)]
         done = 0
         for ring in range(0, rings, 2):
             for pair in range(4):
-                low, high, lowest = patterns[pair]
-                parts = []
-                for offset in range(2):
-                    first = lowest == ring + offset
-                    second = lowest == ring + offset - 1
-                    for sub in range(0, RING, 8):
-                        parts.append(
-                            jnp.where(first, low[sub:sub + 8], jnp.where(second, high[sub:sub + 8], 0.0))
-                        )
-                matrix[ring * RING:(ring + 2) * RING, wide + pair * LANES:wide + (pair + 1) * LANES] = (
-                    jnp.concatenate(parts, axis=0).astype(jnp.bfloat16)
-                )
+                lowest, (here, after, ahead) = patterns[pair]
+                none = jnp.zeros((16, LANES), jnp.bfloat16)
+                for start in range(0, 2 * RING, 16):
+                    rows = slice(start, start + 16)
+                    block = none
+                    if start < RING:
+                        block = jnp.where(lowest == float(ring - 1), ahead[rows], block)
+                    if start + 16 > RING:
+                        block = jnp.where(lowest == float(ring + 1), after[rows], block)
+                    block = jnp.where(lowest == float(ring), here[rows], block)
+                    matrix[ring * RING + start:ring * RING + start + 16,
+                           wide + pair * LANES:wide + (pair + 1) * LANES] = block
             ready = (ring + 2) * RING
             while done < depth and (ready >= done + ROWS or ready == used):
                 size = min(ROWS, depth - done)
@@ -419,7 +426,21 @@
     lane = lax.broadcasted_iota(jnp.int32, (8, LANES), 1)
     copy.wait()
 
-    def bins_step(tile, carry):
+    tiles = -(-per // 8)
+
+    def expanded(tile, column):
+        span = pl.ds(pl.multiple_of(tile * 8, 8), 8)
+        place = starts[column]
+        offset = place & (LANES - 1)
+        start = pl.multiple_of(place - offset, LANES)
+        low = lined[span, pl.ds(start, LANES)]
+        high = lined[span, pl.ds(start + LANES, LANES)]
+        both = jnp.where(lane >= offset, low, high)
+        return jnp.take_along_axis(both, pick[column], axis=1) * sea[column]
+
+    def bins_step(tile, first):
+        following = jnp.minimum(tile + 1, tiles - 1)
+        coming = tuple(expanded(following, column) for column in range(columns))
         span = pl.ds(pl.multiple_of(tile * 8, 8), 8)
         first_bin = jnp.minimum(tile * 8, per - 8)
         tap = [jnp.broadcast_to(taps[span, k:k + 1], (8, LANES)) for k in range(10)]
@@ -432,15 +453,6 @@
         y_left = jnp.where(lane >= 1, tap[6], 0.0)
         y_right = jnp.where(lane < LANES - 1, tap[8], 0.0)
 
-        def expanded(column):
-            place = starts[column]
-            offset = place & (LANES - 1)
-            start = pl.multiple_of(place - offset, LANES)
-            low = lined[span, pl.ds(start, LANES)]
-            high = lined[span, pl.ds(start + LANES, LANES)]
-            both = jnp.where(lane >= offset, low, high)
-            return jnp.take_along_axis(both, pick[column], axis=1) * sea[column]
-
         def store(result, column):
             owner, place = divmod(column - halo, columns_tile)
             start = (owner * per + first_bin) * columns_tile + place
@@ -457,20 +469,17 @@
             return moved * sea[column]
 
         reach = halo // STEPS
-        first = {}
 
         def neighbours(values, column):
             return [values[(column + k) % columns] for k in range(-2, 3)]
 
-        for column in range(columns):
-            first[column] = expanded(column)
         middle = {column: sweep(first, column) for column in range(reach, columns - reach)}
         results = {column: sweep(middle, column) for column in range(halo, columns - halo)}
         for column, result in results.items():
             store(result, column)
-        return carry
-
-    lax.fori_loop(0, -(-per // 8), bins_step, 0)
+        return coming
+
+    lax.fori_loop(0, tiles, bins_step, tuple(expanded(0, column) for column in range(columns)))
 
 
 def propagate(plan, slots, rank, base, got, rel, table):

time: 126 us -> 134 us (1.063)
  blocking collectives: 87.6 us -> 93.9 us
    all_to_all x1, blocking collectives: 52 us -> 58.7 us  [run(): lax.all_to_all(payload[:, :plan.rows(slots)], ('tile', 'bin'), split_axis...]
    pallas_call x1, Pallas kernels: 14.3 us -> 16.1 us  [propagate(): pl.pallas_call(functools.partial(propagate_kernel, plan, slots), out_shap...]
  transfers between devices with their start and end apart: 1 -> 1, of which waited for: 0 -> 0; matrix products, arithmetic and copies ran while one was open for 0% -> 0% of each run, Pallas kernels for 12% -> 11%
where the time goes in v1:
time: 134 us; the launch traced here: 132 us
  blocking collectives  93.9 us (70%)
  Pallas kernels  32 us (24%)
  starting transfers between devices  3 us (2%)
  local copies, waits for them, and re-layouts  1.66 us (1%)
    all_to_all x1, blocking collectives, run(): lax.all_to_all(payload[:, :plan.rows(slots)], ('tile', 'bin'), split_axis...  58.7 us
    all_to_all x1, blocking collectives, shards(): lax.all_to_all(moved.reshape(members, plan.per, plan.columns_tile, latitu...  35.2 us
    pallas_call x1, Pallas kernels, propagate(): pl.pallas_call(functools.partial(propagate_kernel, plan, slots), out_shap...  16.1 us
    pallas_call x1, Pallas kernels, source_terms(): pl.pallas_call(functools.partial(source_kernel, plan), out_shape=jax.Shap...  14.1 us
    ppermute x1, starting transfers between devices, shards(): lax.ppermute(need, 'band', [(band, (band + step) % bands) for band in ran...  3 us
  transfers between devices with their start and end apart: 1, of which 0 were waited for; matrix products, arithmetic and copies ran while one was open for 0% of the time, Pallas kernels for 11%

profile of v1, /device:TPU:0, one launch (start us, length us, event | category | flops | bytes accessed | tf_op | source)
XLA Modules:
  0.0 132.1 jit_solution(11749089971282504983)
XLA Ops:
  0.0 1.7 %sea_ranks.1 = (s32[1]{0:T(128)}, s32[2]{0:T(128)}, s32[1,64]{1,0:T(1,128)S(1)}, s32[64,128]{1,0:T(8,128)S(1)}) custom-call(s32[1]{0:T(128)} %bitcast.rank, s32[64,128]{1,0:T(8,128)} %mask.1, bf16[128,128]{1,0:T(8,128)(2,1)} %constant.63.clone.triangle), custom_call_target="tpu_custom_call" | custom-call | tf_op jit(solution)/shard_map/sea_ranks/pallas_call | solution.py:331
  1.7 3.0 %collective-permute-start = (s32[1]{0:T(128)}, s32[1]{0:T(128)}, u32[]{:S(2)}, u32[]{:S(2)}) collective-permute-start(s32[1]{0:T(128)} %get-tuple-element.122), channel_id=1, source_target_pairs={{0,16},{16,0},{1,17},{17,1},{2,18},{18,2},{3,19},{19,3},{4,20},{20... | collective-permute-start | bytes 20 | tf_op jit(solution)/shard_map/ppermute | solution.py:581
  4.7 0.0 copy-start
  4.7 14.1 %source_terms.1 = f32[16,324,128]{2,1,0:T(8,128)S(1)} custom-call(s32[2]{0:T(128)} %get-tuple-element.123.first_point, f32[1296,256]{1,0:T(8,128)} %spectra_far.1, f32[2,256]{1,0:T(2,128)} %wind_far.1, s32[2,2,4,1296]{3,2,1,0:T(4,128)} %index_far.1, bf16[2,2,4,1296]{3,2,1,0:T(4,128)(2,1)} %weight_far.1, f32[1296]{0:T(1024)} %nl_far.1, ...), custom_call_target="tpu_custom_call" | custom-call | flops 8858370048 | bytes 2654208 | tf_op jit(solution)/shard_map/source_terms/pallas_call | solution.py:262
  18.8 0.0 collective-permute-done
  20.1 0.0 copy-done
  20.2 75.2 %conditional.1 = (f32[5184,128]{1,0:T(8,128)S(1)}) conditional(s32[]{:T(128)} %bitcast.1, (f32[16,324,128]{2,1,0:T(8,128)S(1)}, s32[1]{0:T(128)}, s32[1,64]{1,0:T(1,128)S(1)}, s32[64,128]{1,0:T(8,128)S(1)}, f32[8,168,128]{2,1,0:T(8,128)S(1)}) %tuple.34, (f32[16,324,128]{2,1,0:T(8,128)S(1)}, s32[1]{0:T(128)}, ...), branch_computations={%region_0.1_spmd, %region_1.2_spmd, %region_2.3_spmd, %region_3.4_... | conditional | bytes 10092552 | solution.py:610
  20.4 0.1 slice.15
  20.6 58.7 %all_to_all.36.got = f32[16,276,128]{2,1,0:T(8,128)} all-to-all(f32[16,276,128]{2,1,0:T(8,128)S(1)} %slice.15), channel_id=1, replica_groups=mesh['band'=2,'tile'=8,'bin'=2] {'tile','bin'}, dimensions={0} | all-to-all | bytes 4521984 | tf_op jit(solution)/shard_map/cond/branch_3_fun/all_to_all | solution.py:601
  79.2 16.1 %propagate.10 = f32[5184,128]{1,0:T(8,128)S(1)} custom-call(s32[1]{0:T(128)} %get-tuple-element.98.rank, s32[1,64]{1,0:T(1,128)S(1)} %get-tuple-element.99.base, f32[16,276,128]{2,1,0:T(8,128)} %all_to_all.36.got, s32[64,128]{1,0:T(8,128)S(1)} %get-tuple-element.101.rel, f32[8,168,128]{2,1,0:T(8,128)S(1)} %get-tuple-element.102.table), custom_call_target="tpu_custom_call" | custom-call | tf_op jit(solution)/shard_map/cond/branch_3_fun/propagate/pallas_call | solution.py:491
  95.4 35.2 %all_to_all.40 = f32[4,162,8,128]{3,2,1,0:T(8,128)S(1)} all-to-all(f32[4,162,8,128]{3,2,1,0:T(8,128)S(1)} %bitcast.4), channel_id=1, replica_groups={{0,2,4,6},{8,10,12,14},{1,3,5,7},{9,11,13,15},{16,18,20,22},{24,26,28,3..., dimensions={0} | all-to-all | bytes 5308416 | tf_op jit(solution)/shard_map/all_to_all | solution.py:611
  130.6 1.5 %copy.18 = f32[648,8,128]{2,1,0:T(8,128)} copy(f32[648,8,128]{2,1,0:T(8,128)S(1)} %bitcast.5) | data formatting | bytes 5308416
Async XLA Ops:
  1.7 17.1 %collective-permute-start = (s32[1]{0:T(128)}, s32[1]{0:T(128)}, u32[]{:S(2)}, u32[]{:S(2)}) collective-permute-start(s32[1]{0:T(128)} %get-tuple-element.122), channel_id=1, source_target_pairs={{0,16},{16,0},{1,17},{17,1},{2,18},{18,2},{3,19},{19,3},{4,20},{20... | collective-permute-start | bytes 20 | tf_op jit(solution)/shard_map/ppermute | solution.py:581
  4.7 15.4 %copy-start = (f32[8,168,128]{2,1,0:T(8,128)S(1)}, f32[8,168,128]{2,1,0:T(8,128)}, u32[]{:S(2)}) copy-start(f32[8,168,128]{2,1,0:T(8,128)} %constant.65.clone) | copy-start | bytes 2064388
